TPU v7x, 256 devices: a whole 4x4x8 slice. The times are simulated.
256 devices in a mesh: fsdp: 64 (over z_lo, x, y), tp: 4 (over z_hi, core).
Axes of the slice: x: 4, y: 4, z: 8 (z_hi: 2, z_lo: 4; z = z_hi * 4 + z_lo), core: 2. Of those that a mesh axis runs over, the one named last changes fastest.
Arguments:
- grad_out: bfloat16 [16384, 4096], P('fsdp', 'tp'), may hold values from -16 to 16
- gate_pre: bfloat16 [16384, 14336], P('fsdp', 'tp'), may hold values from -6 to 6
- up_pre: bfloat16 [16384, 14336], P('fsdp', 'tp'), may hold values from -1.5 to 1.5
- down_weight: bfloat16 [4096, 14336], P('fsdp', 'tp'), may hold values from -0.046875 to 0.046875
Outputs:
- grad_gate: bfloat16 [16384, 14336], P('fsdp', 'tp')
- grad_up: bfloat16 [16384, 14336], P('fsdp', 'tp')
- grad_down: bfloat16 [4096, 14336], P('fsdp', 'tp')
All inputs are finite; a program needn't handle non-finite values.
Results may differ from a plain program's by a relative error of at most 0.0049.
Values may be sent and summed in bfloat16 or wider, within the bound.
A program may use at most 320 MiB of HBM per device.

v0:
```python
import jax
import jax.numpy as jnp
from jax import lax
from jax.sharding import PartitionSpec as P


def shards(grad_out, gate_pre, up_pre, down_weight):
    full_cot = lax.all_gather(grad_out, "tp", axis=1, tiled=True)
    gate_val = gate_pre.astype(jnp.float32)
    up_val = up_pre.astype(jnp.float32)
    sigmoid_gate = jax.nn.sigmoid(gate_val)
    swish_gate = gate_val * sigmoid_gate
    hidden = (swish_gate * up_val).astype(jnp.bfloat16)
    grad_hidden = jnp.dot(
        full_cot,
        lax.all_gather(down_weight, "fsdp", axis=0, tiled=True),
        preferred_element_type=jnp.float32,
    )
    grad_gate = (
        grad_hidden * up_val * sigmoid_gate * (1.0 + gate_val * (1.0 - sigmoid_gate))
    ).astype(jnp.bfloat16)
    grad_up = (grad_hidden * swish_gate).astype(jnp.bfloat16)
    weight_term = lax.dot_general(
        full_cot, hidden, (((0,), (0,)), ((), ())), preferred_element_type=jnp.float32
    )
    summed = lax.psum_scatter(weight_term, "fsdp", scatter_dimension=0, tiled=True)
    return (grad_gate, grad_up, summed.astype(jnp.bfloat16))


def solution(mesh):
    return jax.shard_map(
        shards,
        mesh=mesh,
        in_specs=(P("fsdp", "tp"), P("fsdp", "tp"), P("fsdp", "tp"), P("fsdp", "tp")),
        out_specs=(P("fsdp", "tp"), P("fsdp", "tp"), P("fsdp", "tp")),
        check_vma=False,
    )
```

profile of v0, /device:TPU:96, one launch (start us, length us, event | category | flops | bytes accessed | tf_op | source)
XLA Modules:
  0.0 1103.6 jit_solution(11518910066108114450)
XLA Ops:
  7.2 0.0 all-gather.3.cloned.1.call-start
  7.2 0.7 all-gather.3.cloned.1.call-update
  7.9 0.0 all-gather.5.cloned.1.call-start
  7.9 0.7 all-gather.5.cloned.1.call-update
  8.6 0.0 reduce-scatter.4.cloned.1.call-start
  8.7 43.5 %all-gather.3.cloned.1.call-done = bf16[256,4096]{1,0:T(8,128)(2,1)} async-done(((bf16[256,1024]{1,0:T(8,128)(2,1)}), bf16[256,4096]{1,0:T(8,128)(2,1)}) %all-gather.3.cloned.1.call-update) | async-done | bytes 2097168 | tf_op jit(solution)/shard_map/all_gather | solution.py:8
  52.2 24.5 %convolution_bitcast_fusion = f32[4096,3584]{0,1:T(8,128)} fusion(bf16[256,4096]{1,0:T(8,128)(2,1)} %all-gather.3.cloned.1.call-done, bf16[256,3584]{1,0:T(8,128)(2,1)} %param.6, bf16[256,3584]{1,0:T(8,128)(2,1)} %param.5), kind=kOutput, calls=%fused_computation | convolution fusion | flops 7523532800 | bytes 64487424 | tf_op jit(solution)/shard_map/dot_general | solution.py:23
  76.7 54.7 %copy.9 = f32[4096,3584]{1,0:T(8,128)} copy(f32[4096,3584]{0,1:T(8,128)} %convolution_bitcast_fusion) | data formatting | bytes 117440512
  131.4 0.0 copy-start
  131.4 0.0 reduce-scatter.4.cloned.1.call-update
  131.4 296.2 %all-gather.5.cloned.1.call-done = bf16[4096,3584]{1,0:T(8,128)(2,1)} async-done(((bf16[64,3584]{1,0:T(8,128)(2,1)}), bf16[4096,3584]{1,0:T(8,128)(2,1)}) %all-gather.5.cloned.1.call-update) | async-done | bytes 29360144 | tf_op jit(solution)/shard_map/all_gather | solution.py:16
  427.6 0.0 copy-done
  427.6 16.0 %multiply_convert_fusion = (bf16[256,3584]{1,0:T(8,128)(2,1)}, bf16[256,3584]{1,0:T(8,128)(2,1)}) fusion(bf16[256,3584]{1,0:T(8,128)(2,1)S(1)} %copy-done, bf16[256,3584]{1,0:T(8,128)(2,1)} %param.6, bf16[256,4096]{1,0:T(8,128)(2,1)} %all-gather.3.cloned.1.call-done, bf16[4096,3584]{1,0:T(8,128)(2,1)} %all-gather.5.cloned.1.call-done), kind=kOutput, calls=%fused_computation.14 | convolution fusion | flops 7529955328 | bytes 38797312 | tf_op jit(solution)/shard_map/dot_general | solution.py:14
  443.6 650.8 %reduce-scatter.4.cloned.1.call-done = f32[64,3584]{1,0:T(8,128)} async-done(((f32[4096,3584]{1,0:T(8,128)}), f32[64,3584]{1,0:T(8,128)}) %reduce-scatter.4.cloned.1.call-update) | async-done | bytes 917520
  1094.4 1.6 copy.10
  1096.0 1.1 copy.8
Async XLA Ops:
  7.2 45.0 %all-gather.3.cloned.1.call-start = ((), (), s32[]{:S(2)}) async-start(), calls=%async_computation.1 | async-start | bytes 2621440 | tf_op jit(solution)/shard_map/all_gather | solution.py:8
  7.9 419.7 %all-gather.5.cloned.1.call-start = ((), (), s32[]{:S(2)}) async-start(), calls=%async_computation.2 | async-start | bytes 29818880 | tf_op jit(solution)/shard_map/all_gather | solution.py:16
  8.6 1085.7 %reduce-scatter.4.cloned.1.call-start = ((), (), s32[]{:S(2)}) async-start(), calls=%async_computation.3 | async-start | bytes 59637760
  131.4 296.2 %copy-start = (bf16[256,3584]{1,0:T(8,128)(2,1)S(1)}, bf16[256,3584]{1,0:T(8,128)(2,1)}, u32[]{:S(2)}) copy-start(bf16[256,3584]{1,0:T(8,128)(2,1)} %param.5) | copy-start | bytes 5505028
Sparse Core Ops, SparseCore 0:
  9.8 42.3 all-gather.2
  54.0 373.6 all-gather.4
  430.2 664.1 reduce-scatter.3
where the time goes:
time: 1110 us; the launch traced here: 1100 us
  waiting for transfers between devices  992 us (89%)
  local copies, waits for them, and re-layouts  57.4 us (5%)
  matrix products  40.5 us (4%)
  between operations  13.8 us (1%)
    unnamed x4, waiting for transfers between devices  652 us
    all_gather x1, waiting for transfers between devices, shards(): lax.all_gather(down_weight, 'fsdp', axis=0, tiled=True)  296 us
    unnamed x5, local copies, waits for them, and re-layouts  57.4 us
    all_gather x1, waiting for transfers between devices, shards(): full_cot = lax.all_gather(grad_out, 'tp', axis=1, tiled=True)  43.5 us
    dot_general x1, matrix products, shards(): lax.dot_general(full_cot, hidden, (((0,), (0,)), ((), ())), preferred_ele...  24.5 us
  transfers between devices with their start and end apart: 3, of which 3 were waited for; matrix products, arithmetic and copies ran while one was open for 9% of the time, Pallas kernels for 0%

commit v1 on v0

v1 whole, which is shorter than its diff:
```python
import functools

import jax
import jax.numpy as jnp
from jax import lax
from jax.experimental import pallas as pl
from jax.experimental.pallas import tpu as pltpu
from jax.sharding import Mesh, PartitionSpec as P

AXES = ("zl", "x", "y", "zh", "c")
BF = jnp.bfloat16
F32 = jnp.float32


def dot(a, b):
    return lax.dot_general(a, b, (((1,), (0,)), ((), ())), preferred_element_type=F32)


def kernel(
    T, D, FB, DB,
    go_in, gate_in, up_in, w_in,
    gg_out, gu_out, gd_out,
    go, w, gate, up, ht, gh, ggs, gus, acc,
    far_s, far_r, near_s, near_r, z_s, z_r, fin,
    ssem, rsem, lsem,
):
    zl, x, y, zh, c = (lax.axis_index(a) for a in AXES)
    half_t, half_f, half_d = T // 2, FB // 2, DB // 2
    rows_w = DB // 4

    def al(v, m):
        return pl.multiple_of(v, m)

    def at(dz=0, dx=0, dy=0, dh=0, dc=0):
        return ((zl + dz) % 4, (x + dx) % 4, (y + dy) % 4, (zh + dh) % 2, (c + dc) % 2)

    ids = {}
    sends = []

    def rcopy(key, src, dst, dev, sem=None):
        i = ids.setdefault(key, len(ids)) if sem is None else sem
        cp = pltpu.make_async_remote_copy(
            src_ref=src, dst_ref=dst, send_sem=ssem.at[i], recv_sem=rsem.at[i],
            device_id=dev, device_id_type=pl.DeviceIdType.MESH,
        )
        return cp

    def send(key, src, dst, dev):
        cp = rcopy(key, src, dst, dev)
        cp.start()
        sends.append(cp)
        return cp

    nloc = [0]

    def lcopy(src, dst):
        cp = pltpu.make_async_copy(src, dst, lsem.at[nloc[0]])
        nloc[0] += 1
        cp.start()
        return cp

    partners = [at(dy=1), at(dy=2), at(dy=3), at(dx=1), at(dx=3),
                at(dz=1), at(dz=2), at(dz=3), at(dh=1), at(dc=1)]
    bar = pltpu.get_barrier_semaphore()
    for p in partners:
        pl.semaphore_signal(bar, inc=1, device_id=p, device_id_type=pl.DeviceIdType.MESH)
    pl.semaphore_wait(bar, len(partners))

    def fcols(yy):
        return pl.ds(al((yy % 4) * FB, 128), FB)

    def wrows(zz, xx, off=0, n=None):
        return pl.ds(al(((zz % 4) * 4 + xx % 4) * DB + off, 16), DB if n is None else n)

    def trows(yy, off=0, n=None):
        return pl.ds(al((yy % 4) * T + off, 16), T if n is None else n)

    my_w = pl.ds(al(((zl * 4 + x) * 4 + y) * rows_w, 16), rows_w)
    wy = [send(("wy", j), w_in.at[:, fcols(y + j)], w.at[my_w, :], at(dy=j)) for j in (1, 3, 2)]
    wl = lcopy(w_in.at[:, fcols(y)], w.at[my_w, :])

    def quarter(s):
        return 2 * ((zh + s % 2) % 2) + (c + s // 2) % 2

    def gblock(s, dy, off=0, n=None):
        return go.at[trows(y + dy, off, n), pl.ds(al(quarter(s) * D, 128), D)]

    gl = lcopy(go_in, gblock(0, 0))
    gz = send("gz", go_in, gblock(0, 0), at(dh=1))
    gc00 = send(("gc", 0, 0), go_in, gblock(0, 0), at(dc=1))
    gu = {}
    for j in (1, 3, 2):
        gu[j] = (
            send(("gate", j), gate_in.at[:, fcols(y + j)], gate.at[trows(y), :], at(dy=j)),
            send(("up", j), up_in.at[:, fcols(y + j)], up.at[trows(y), :], at(dy=j)),
        )
    gul = (lcopy(gate_in.at[:, fcols(y)], gate.at[trows(y), :]),
           lcopy(up_in.at[:, fcols(y)], up.at[trows(y), :]))

    w1 = {}
    w2 = {}

    def w_x_sends(k):
        blk = w.at[wrows(zl - k, x), :]
        w1[k] = (send(("w1p", k), blk, blk, at(dx=1)), send(("w1m", k), blk, blk, at(dx=3)))

    def w_x_forward(k):
        w1[k][0].wait_recv()
        lo = w.at[wrows(zl - k, x - 1, 0, half_d), :]
        a = send(("w2p", k), lo, lo, at(dx=1))
        w1[k][1].wait_recv()
        hi = w.at[wrows(zl - k, x + 1, half_d, half_d), :]
        b = send(("w2m", k), hi, hi, at(dx=3))
        w2[k] = (a, b)

    g1 = {}
    g2 = {}
    gcs = [gc00]

    def g_y_sends(s):
        blk = gblock(s, 0)
        g1[s] = (send(("g1p", s), blk, blk, at(dy=1)), send(("g1m", s), blk, blk, at(dy=3)))

    def g_core(s, tag, blk):
        gcs.append(send(("gc", s, tag), blk, blk, at(dc=1)))

    def g_y_forward(s):
        g1[s][0].wait_recv()
        lo = gblock(s, -1, 0, half_t)
        a = send(("g2p", s), lo, lo, at(dy=1))
        g_core(s, 1, gblock(s, -1))
        g1[s][1].wait_recv()
        hi = gblock(s, 1, half_t, half_t)
        b = send(("g2m", s), hi, hi, at(dy=3))
        g_core(s, 3, gblock(s, 1))
        g2[s] = (a, b)

    def g_y_last(s):
        g2[s][0].wait_recv()
        g_core(s, 4, gblock(s, 2, 0, half_t))
        g2[s][1].wait_recv()
        g_core(s, 5, gblock(s, 2, half_t, half_t))

    def hidden(yy):
        r0 = trows(yy)

        @pl.loop(0, FB // 128)
        def _(i):
            cs = pl.ds(al(i * 128, 128), 128)
            g = gate[r0, cs].astype(F32)
            u = up[r0, cs].astype(F32)
            h = g * jax.nn.sigmoid(g) * u
            ht[cs, r0] = h.T.astype(BF)

    wl.wait()
    for cp in wy:
        cp.wait_recv()
    own_w = w.at[wrows(zl, x), :]
    wz = {j: send(("wz", j), own_w, own_w, at(dz=j)) for j in (1, 3, 2)}
    w_x_sends(0)
    for cp in gul:
        cp.wait()
    hidden(y)
    gl.wait()
    w_x_forward(0)
    wz[1].wait_recv()
    w_x_sends(1)
    for cp in gu[1]:
        cp.wait_recv()
    g_y_sends(0)
    hidden(y - 1)
    gz.wait_recv()
    g_core(1, 0, gblock(1, 0))
    w_x_forward(1)
    wz[3].wait_recv()
    w_x_sends(3)
    for cp in gu[3]:
        cp.wait_recv()
    g_y_sends(1)
    hidden(y - 3)
    w_x_forward(3)
    wz[2].wait_recv()
    w_x_sends(2)
    for cp in gu[2]:
        cp.wait_recv()
    hidden(y - 2)
    g_y_forward(0)
    w_x_forward(2)
    g_y_forward(1)
    g_y_last(0)
    g_y_last(1)
    for cp in gcs:
        cp.wait_recv()

    nst = len(ids)

    def part(i, dx, h0, n):
        col = al((((zl + 1 + i) % 4) * 4 + (x + dx) % 4) * DB, 128)
        return dot(ht[pl.ds(h0, n), :], go[:, pl.ds(col, DB)])

    def far_copies(i):
        return (
            rcopy(None, far_s.at[i, 0], far_r.at[i, 0], at(dx=1), nst + i),
            rcopy(None, far_s.at[i, 1], far_r.at[i, 1], at(dx=3), nst + 4 + i),
        )

    def near_copies(i):
        return (
            rcopy(None, near_s.at[i, 0], near_r.at[i, 0], at(dx=1), nst + 8 + i),
            rcopy(None, near_s.at[i, 1], near_r.at[i, 1], at(dx=3), nst + 12 + i),
        )

    def far(i):
        cps = far_copies(i)
        for k in range(2):
            far_s[i, k] = part(i, 2, k * half_f, half_f).astype(BF)
            cps[k].start()

    def near(i):
        fcps = far_copies(i)
        cps = near_copies(i)
        for k, dx in ((0, 1), (1, 3)):
            o = 1 - k
            near_s[i, k, pl.ds(o * half_f, half_f), :] = part(i, dx, o * half_f, half_f).astype(BF)
            p = part(i, dx, k * half_f, half_f)
            fcps[k].wait_recv()
            near_s[i, k, pl.ds(k * half_f, half_f), :] = (p + far_r[i, k].astype(F32)).astype(BF)
            cps[k].start()

    def own(i):
        cps = near_copies(i)
        for cp in cps:
            cp.wait_recv()
        for k in range(2):
            r = pl.ds(k * half_f, half_f)
            acc[r, :] = (part(i, 0, k * half_f, half_f) + near_r[i, 0, r, :].astype(F32)
                         + near_r[i, 1, r, :].astype(F32))

    def z_copy(i):
        return rcopy(None, z_s.at[i], z_r.at[i], at(dz=1 + i), nst + 16 + i)

    outs = []

    def out_copies(t):
        j = (2, 1, 3)[t]
        return (
            rcopy(None, ggs.at[t], gg_out.at[:, fcols(y)], at(dy=j), nst + 19 + t),
            rcopy(None, gus.at[t], gu_out.at[:, fcols(y)], at(dy=j), nst + 22 + t),
        )

    def grad_in(t):
        yy = y + (2, 1, 3, 0)[t]
        r0 = al((yy % 4) * T, 16)
        gh[...] = dot(go[pl.ds(r0, T), :], w[...])

        @pl.loop(0, T // 32)
        def _(i):
            r = pl.ds(al(i * 32, 16), 32)
            rr = pl.ds(al(r0 + i * 32, 16), 32)
            g = gate[rr, :].astype(F32)
            u = up[rr, :].astype(F32)
            s = jax.nn.sigmoid(g)
            d = gh[r, :]
            ggs[t, r, :] = (d * u * s * (1.0 + g * (1.0 - s))).astype(BF)
            gus[t, r, :] = (d * (g * s)).astype(BF)

        if t < 3:
            for cp in out_copies(t):
                cp.start()
        else:
            outs.append(lcopy(ggs.at[t], gg_out.at[:, fcols(y)]))
            outs.append(lcopy(gus.at[t], gu_out.at[:, fcols(y)]))

    def own_z(i):
        own(i)
        z_s[i] = acc[...].astype(BF)
        z_copy(i).start()

    far(0)
    far(1)
    near(0)
    for k in (0, 1, 3, 2):
        for cp in w2[k]:
            cp.wait_recv()
    grad_in(0)
    far(2)
    near(1)
    own_z(0)
    grad_in(1)
    far(3)
    near(2)
    own_z(1)
    grad_in(2)
    near(3)
    own_z(2)
    grad_in(3)
    own(3)
    for i in range(3):
        z_copy(i).wait_recv()

    @pl.loop(0, FB // 128)
    def _(i):
        r = pl.ds(al(i * 128, 128), 128)
        tot = acc[r, :] + z_r[0, r, :].astype(F32) + z_r[1, r, :].astype(F32) + z_r[2, r, :].astype(F32)
        fin[:, r] = tot.T.astype(BF)

    def drows(yy):
        return pl.ds(al((yy % 4) * rows_w, 16), rows_w)

    fcp = []
    for t, j in enumerate((2, 1, 3)):
        cp = rcopy(None, fin.at[drows(y + j), :], gd_out.at[:, fcols(y)], at(dy=j), nst + 25 + t)
        cp.start()
        fcp.append(cp)
    outs.append(lcopy(fin.at[drows(y), :], gd_out.at[:, fcols(y)]))

    for cp in sends:
        cp.wait_send()
    for i in range(4):
        for cp in far_copies(i) + near_copies(i):
            cp.wait_send()
    for i in range(3):
        z_copy(i).wait_send()
        for cp in out_copies(i):
            cp.wait()
        fcp[i].wait()
    for cp in outs:
        cp.wait()


def shards(go, gate, up, w):
    T, D = go.shape
    F = gate.shape[1]
    FB, DB = F // 4, w.shape[0] * 4
    vm = lambda *s: pltpu.VMEM(s, BF)
    return pl.pallas_call(
        functools.partial(kernel, T, D, FB, DB),
        out_shape=(
            jax.ShapeDtypeStruct((T, F), BF),
            jax.ShapeDtypeStruct((T, F), BF),
            jax.ShapeDtypeStruct(w.shape, BF),
        ),
        in_specs=[pl.BlockSpec(memory_space=pl.ANY)] * 4,
        out_specs=(pl.BlockSpec(memory_space=pl.ANY),) * 3,
        scratch_shapes=[
            vm(4 * T, 4 * D), vm(16 * DB, FB), vm(4 * T, FB), vm(4 * T, FB), vm(FB, 4 * T),
            pltpu.VMEM((T, FB), F32), vm(4, T, FB), vm(4, T, FB), pltpu.VMEM((FB, DB), F32),
            vm(4, 2, FB // 2, DB), vm(4, 2, FB // 2, DB), vm(4, 2, FB, DB), vm(4, 2, FB, DB),
            vm(3, FB, DB), vm(3, FB, DB), vm(DB, FB),
            pltpu.SemaphoreType.DMA((96,)), pltpu.SemaphoreType.DMA((96,)), pltpu.SemaphoreType.DMA((12,)),
        ],
        compiler_params=pltpu.CompilerParams(
            collective_id=0, has_side_effects=True, vmem_limit_bytes=58 << 20
        ),
        cost_estimate=pl.CostEstimate(
            flops=4 * 4 * T * 4 * D * FB, bytes_accessed=12 * T * F, transcendentals=2 * T * F
        ),
        name="regrouped_backward",
    )(go, gate, up, w)


def solution(mesh):
    fine = Mesh(mesh.devices.reshape(4, 4, 4, 2, 2), AXES)
    spec = P(("zl", "x", "y"), ("zh", "c"))
    return jax.shard_map(
        shards, mesh=fine, in_specs=(spec,) * 4, out_specs=(spec,) * 3, check_vma=False
    )
```

time: 1110 us -> 180 us (0.16)
  waiting for transfers between devices: 992 us -> 0 us
  Pallas kernels: 0 us -> 172 us
  local copies, waits for them, and re-layouts: 57.4 us -> 5.08 us
  matrix products: 40.5 us -> 0 us
  between operations: 13.8 us -> 0.65 us
    unnamed x4 -> x0, waiting for transfers between devices: 652 us -> none
    all_gather x2 -> x0, waiting for transfers between devices: 340 us -> none  [the longest x1 296 us: shards(): lax.all_gather(down_weight, 'fsdp', axis=0, tiled=True)]
    pallas_call x0 -> x1, Pallas kernels: none -> 172 us  [shards(): pl.pallas_call(functools.partial(kernel, T, D, FB, DB), out_shape=(jax.Sh...]
    unnamed x5 -> x7, local copies, waits for them, and re-layouts: 57.4 us -> 5.08 us
    dot_general x2 -> x0, matrix products: 40.5 us -> none  [the longest x1 24.5 us: shards(): lax.dot_general(full_cot, hidden, (((0,), (0,)), ((), ())), preferred_ele...]
  transfers between devices with their start and end apart: 3 -> 0, of which waited for: 3 -> 0; matrix products, arithmetic and copies ran while one was open for 9% -> 0% of each run, Pallas kernels for 0% -> 0%
where the time goes in v1:
time: 180 us; the launch traced here: 178 us
  Pallas kernels  172 us (96%)
  local copies, waits for them, and re-layouts  5.08 us (3%)
    pallas_call x1, Pallas kernels, shards(): pl.pallas_call(functools.partial(kernel, T, D, FB, DB), out_shape=(jax.Sh...  172 us
    unnamed x7, local copies, waits for them, and re-layouts  5.08 us

profile of v1, /device:TPU:96, one launch (start us, length us, event | category | flops | bytes accessed | tf_op | source)
XLA Modules:
  0.0 177.5 jit_solution(14681745384588799466)
XLA Ops:
  0.6 171.8 %regrouped_backward.1 = (bf16[256,3584]{1,0:T(8,128)(2,1)}, bf16[256,3584]{1,0:T(8,128)(2,1)}, bf16[64,3584]{1,0:T(8,128)(2,1)}) custom-call(bf16[256,1024]{1,0:T(8,128)(2,1)} %go_in.1, bf16[256,3584]{1,0:T(8,128)(2,1)} %gate_in.1, bf16[256,3584]{1,0:T(8,128)(2,1)} %up_in.1, bf16[64,3584]{1,0:T(8,128)(2,1)} %w_in.1), custom_call_target="tpu_custom_call" | custom-call | flops 15032385536 | bytes 11010048 | tf_op jit(solution)/shard_map/regrouped_backward/pallas_call | solution.py:336
  172.4 0.0 copy-start
  172.4 3.0 %copy.10 = bf16[256,3584]{1,0:T(8,128)(2,1)} copy(bf16[256,3584]{1,0:T(8,128)(2,1)} %get-tuple-element.6) | data formatting | bytes 3670016
  175.4 0.0 copy-done
  175.4 0.0 copy-start.1
  175.4 1.2 copy.11
  176.6 0.1 copy-done.1
  176.7 0.8 copy.12
Async XLA Ops:
  172.4 3.0 %copy-start = (bf16[256,3584]{1,0:T(8,128)(2,1)S(1)}, bf16[256,3584]{1,0:T(8,128)(2,1)}, u32[]{:S(2)}) copy-start(bf16[256,3584]{1,0:T(8,128)(2,1)} %get-tuple-element.7) | copy-start | bytes 5505028
  175.4 1.3 copy-start.1

commit v2 on v1

v2 whole, which is shorter than its diff:
```python
import functools

import jax
import jax.numpy as jnp
from jax import lax
from jax.experimental import pallas as pl
from jax.experimental.pallas import tpu as pltpu
from jax.sharding import Mesh, PartitionSpec as P

AXES = ("zl", "x", "y", "zh", "c")
BF = jnp.bfloat16
F32 = jnp.float32


def dot(a, b):
    return lax.dot_general(a, b, (((1,), (0,)), ((), ())), preferred_element_type=F32)


def kernel(
    T, D, FB, DB,
    go_in, gate_in, up_in, w_in,
    gg_out, gu_out, gd_out,
    go, w, gate, up, ht, gh, ggs, gus, acc,
    far_s, far_r, near_s, near_r, z_s, z_r, fin,
    ssem, rsem, lsem,
):
    zl, x, y, zh, c = (lax.axis_index(a) for a in AXES)
    half_t, half_f, half_d = T // 2, FB // 2, DB // 2
    rows_w = DB // 4

    def al(v, m):
        return pl.multiple_of(v, m)

    def at(dz=0, dx=0, dy=0, dh=0, dc=0):
        return ((zl + dz) % 4, (x + dx) % 4, (y + dy) % 4, (zh + dh) % 2, (c + dc) % 2)

    ids = {}
    sends = []

    def rcopy(src, dst, dev, i, j=None):
        return pltpu.make_async_remote_copy(
            src_ref=src, dst_ref=dst, send_sem=ssem.at[i], recv_sem=rsem.at[i if j is None else j],
            device_id=dev, device_id_type=pl.DeviceIdType.MESH,
        )

    def send(key, src, dst, dev):
        cp = rcopy(src, dst, dev, ids.setdefault(key, len(ids)))
        cp.start()
        sends.append(cp)
        return cp

    nloc = [0]

    def lcopy(src, dst):
        cp = pltpu.make_async_copy(src, dst, lsem.at[nloc[0]])
        nloc[0] += 1
        cp.start()
        return cp

    partners = [at(dy=1), at(dy=2), at(dy=3), at(dx=1), at(dx=3),
                at(dz=1), at(dz=2), at(dz=3), at(dh=1), at(dc=1)]
    bar = pltpu.get_barrier_semaphore()
    for p in partners:
        pl.semaphore_signal(bar, inc=1, device_id=p, device_id_type=pl.DeviceIdType.MESH)
    pl.semaphore_wait(bar, len(partners))

    def fcols(yy):
        return pl.ds(al((yy % 4) * FB, 128), FB)

    def wrows(zz, xx, k=None):
        off, n = (0, DB) if k is None else (k * half_d, half_d)
        return pl.ds(al(((zz % 4) * 4 + xx % 4) * DB + off, 16), n)

    def trows(yy, k=None):
        off, n = (0, T) if k is None else (k * half_t, half_t)
        return pl.ds(al((yy % 4) * T + off, 16), n)

    def quarter(s):
        return 2 * ((zh + s % 2) % 2) + (c + s // 2) % 2

    def gblock(s, dy, k=None):
        return go.at[trows(y + dy, k), pl.ds(al(quarter(s) * D, 128), D)]

    my_w = pl.ds(al(((zl * 4 + x) * 4 + y) * rows_w, 16), rows_w)
    wy = [send(("wy", j), w_in.at[:, fcols(y + j)], w.at[my_w, :], at(dy=j)) for j in (1, 3, 2)]
    wl = lcopy(w_in.at[:, fcols(y)], w.at[my_w, :])
    gul = (lcopy(gate_in.at[:, fcols(y)], gate.at[trows(y), :]),
           lcopy(up_in.at[:, fcols(y)], up.at[trows(y), :]))
    gl = lcopy(go_in, gblock(0, 0))
    gu = {}
    for j in (1, 3, 2):
        gu[j] = (
            send(("gate", j), gate_in.at[:, fcols(y + j)], gate.at[trows(y), :], at(dy=j)),
            send(("up", j), up_in.at[:, fcols(y + j)], up.at[trows(y), :], at(dy=j)),
        )
    gcs = [send(("gc", 0, 0), go_in, gblock(0, 0), at(dc=1))]

    def ring_sends(tag, ref, axis):
        out = {}
        for k in (0, 1):
            out[0, k] = send((tag, "p", k), ref(0, k), ref(0, k), at(**{axis: 1}))
            out[1, k] = send((tag, "m", k), ref(0, 1 - k), ref(0, 1 - k), at(**{axis: 3}))
        return out

    def ring_forward(tag, ref, axis, first):
        first[0, 0].wait_recv()
        a = send((tag, "fp"), ref(-1, 0), ref(-1, 0), at(**{axis: 1}))
        first[1, 0].wait_recv()
        b = send((tag, "fm"), ref(1, 1), ref(1, 1), at(**{axis: 3}))
        return (first[0, 1], first[1, 1], a, b)

    def zsrc(k):
        return (zl, zl + 1 - 2 * (zl % 2), 2 - zl // 2, 3 - 3 * (zl // 2))[k]

    def w_ref(k):
        return lambda dx, h: w.at[wrows(zsrc(k), x + dx, h), :]

    def g_ref(s):
        return lambda dy, h: go.at[trows(y + dy, h), pl.ds(al(quarter(s) * D, 128), D)]

    w1, w2, g1, g2 = {}, {}, {}, {}

    def w_x_sends(k):
        w1[k] = ring_sends(("w", k), w_ref(k), "dx")

    def w_x_forward(k):
        w2[k] = ring_forward(("w", k), w_ref(k), "dx", w1[k])

    def g_y_sends(s):
        g1[s] = ring_sends(("g", s), g_ref(s), "dy")

    def g_y_forward(s):
        g2[s] = ring_forward(("g", s), g_ref(s), "dy", g1[s])

    def g_core(s, tag, blk):
        gcs.append(send(("gc", s, tag), blk, blk, at(dc=1)))

    def g_core_near(s):
        g2[s][0].wait_recv()
        g_core(s, 1, gblock(s, -1))
        g2[s][1].wait_recv()
        g_core(s, 3, gblock(s, 1))

    def g_core_far(s):
        g2[s][2].wait_recv()
        g_core(s, 4, gblock(s, 2, 0))
        g2[s][3].wait_recv()
        g_core(s, 5, gblock(s, 2, 1))

    def hidden(yy):
        r0 = trows(yy)

        @pl.loop(0, FB // 128)
        def _(i):
            cs = pl.ds(al(i * 128, 128), 128)
            g = gate[r0, cs].astype(F32)
            u = up[r0, cs].astype(F32)
            h = g * jax.nn.sigmoid(g) * u
            ht[cs, r0] = h.T.astype(BF)

    wl.wait()
    for cp in wy:
        cp.wait_recv()
    w_x_sends(0)
    zr0 = len(ids)
    for k in range(11):
        ids["wz", k] = len(ids)
    zwhen = []

    def z_w_send(src, dest, i, j, cond):
        blk = w.at[wrows(src, x), :]
        cp = rcopy(blk, blk, (dest, x, y, zh, c), zr0 + i, zr0 + j)

        @pl.when(cond)
        def _():
            cp.start()

        zwhen.append((cond, cp))

    z_w_send(zl, (zl + 1) % 4, 6, 3, zl < 3)
    z_w_send(zl, (zl + 3) % 4, 7, 0, zl > 0)

    def z_w_slot(k):
        src = zsrc(k)
        r = (src - zl + 4) // 4
        step = (src - zl) * (2 * r - 1)
        j = 3 * (1 - r) + step
        blk = w.at[wrows(src, x), :]
        rcopy(blk, blk, at(dz=1), zr0, zr0 + j - 1).wait_recv()
        dest = zl + 1 - 2 * r
        z_w_send(src, (dest + 4) % 4, 7 + k, j % 6, (dest >= 0) & (dest <= 3))

    gz = [send(("gz", 0), go_in.at[pl.ds(0, half_t), :], gblock(0, 0, 0), at(dh=1))]
    gl.wait()
    g_y_sends(0)
    for cp in gul:
        cp.wait()
    hidden(y)
    w_x_forward(0)
    z_w_slot(1)
    w_x_sends(1)
    z_w_slot(2)
    w_x_sends(2)
    gz.append(send(("gz", 1), go_in.at[pl.ds(half_t, half_t), :], gblock(0, 0, 1), at(dh=1)))
    w_x_forward(1)
    for cp in gu[1]:
        cp.wait_recv()
    hidden(y - 1)
    for cp in gu[3]:
        cp.wait_recv()
    hidden(y - 3)
    z_w_slot(3)
    w_x_sends(3)
    w_x_forward(2)
    for cp in gu[2]:
        cp.wait_recv()
    hidden(y - 2)
    g_y_forward(0)
    w_x_forward(3)
    for cp in gz:
        cp.wait_recv()
    g_y_sends(1)
    g_core_near(0)
    g_core(1, 0, gblock(1, 0))
    g_core_far(0)
    for cp in (gcs[i] for i in (0, 1, 2, 4, 5)):
        cp.wait_recv()

    nst = 72
    same = (zh + zl // 2 + 1) % 2
    z1, z2, z3 = zl + 1 - 2 * (zl % 2), (zl + 2) % 4, 3 - zl
    order = (same * z1 + (1 - same) * z2, z3, same * z2 + (1 - same) * z1, zl)

    def part(i, dx, h0, n):
        col = al((order[i] * 4 + (x + dx) % 4) * DB, 128)
        return dot(ht[pl.ds(h0, n), :], go[:, pl.ds(col, DB)])

    def half(k):
        return pl.ds(k * half_f, half_f)

    def far_copies(i):
        return [rcopy(far_s.at[i, k], far_r.at[i, k], at(dx=1 + 2 * k), nst + 2 * i + k) for k in range(2)]

    def near_copies(i):
        return [[rcopy(near_s.at[i, k, half(h)], near_r.at[i, k, half(h)], at(dx=1 + 2 * k),
                       nst + 8 + 4 * i + 2 * k + h) for h in range(2)] for k in range(2)]

    def far(i):
        cps = far_copies(i)
        for k in range(2):
            far_s[i, k] = part(i, 2, k * half_f, half_f).astype(BF)
            cps[k].start()

    def near_own(i):
        cps = near_copies(i)
        for k in range(2):
            h = 1 - k
            near_s[i, k, half(h), :] = part(i, 1 + 2 * k, h * half_f, half_f).astype(BF)
            cps[k][h].start()

    def near_far(i):
        fcps = far_copies(i)
        cps = near_copies(i)
        for k in range(2):
            p = part(i, 1 + 2 * k, k * half_f, half_f)
            fcps[k].wait_recv()
            near_s[i, k, half(k), :] = (p + far_r[i, k].astype(F32)).astype(BF)
            cps[k][k].start()

    def own_part(i, extra=()):
        for h in range(2):
            t = part(i, 0, h * half_f, half_f)
            for e in extra:
                t = t + z_r[e, half(h), :].astype(F32)
            acc[half(h), :] = t

    def near_wait(i, h):
        for k in range(2):
            near_copies(i)[k][h].wait_recv()

    def z_copy(i):
        off = (order[i] - zl) % 4 - 1
        return rcopy(z_s.at[i], z_r.at[off], (order[i], x, y, zh, c), nst + 24 + i, nst + 24 + off)

    def own_z(i):
        own_part(i)
        for h in range(2):
            near_wait(i, h)
            z_s[i, half(h), :] = (acc[half(h), :] + near_r[i, 0, half(h), :].astype(F32)
                                  + near_r[i, 1, half(h), :].astype(F32)).astype(BF)
        z_copy(i).start()

    outs = []

    def out_copies(t):
        j = (2, 1, 3)[t]
        return (
            rcopy(ggs.at[t], gg_out.at[:, fcols(y)], at(dy=j), nst + 27 + t),
            rcopy(gus.at[t], gu_out.at[:, fcols(y)], at(dy=j), nst + 30 + t),
        )

    def grad_in(t):
        yy = y + (2, 1, 3, 0)[t]
        r0 = al((yy % 4) * T, 16)
        gh[...] = dot(go[pl.ds(r0, T), :], w[...])

        @pl.loop(0, T // 32)
        def _(i):
            r = pl.ds(al(i * 32, 16), 32)
            rr = pl.ds(al(r0 + i * 32, 16), 32)
            g = gate[rr, :].astype(F32)
            u = up[rr, :].astype(F32)
            s = jax.nn.sigmoid(g)
            d = gh[r, :]
            ggs[t, r, :] = (d * u * s * (1.0 + g * (1.0 - s))).astype(BF)
            gus[t, r, :] = (d * (g * s)).astype(BF)

        if t < 3:
            for cp in out_copies(t):
                cp.start()
        else:
            outs.append(lcopy(ggs.at[t], gg_out.at[:, fcols(y)]))
            outs.append(lcopy(gus.at[t], gu_out.at[:, fcols(y)]))

    far(0)
    near_own(0)
    g_y_forward(1)
    near_far(0)
    g_core_near(1)
    g_core_far(1)
    for cp in (gcs[i] for i in (3, 6, 7, 8, 9)):
        cp.wait_recv()
    far(1)
    near_own(1)
    for k in range(4):
        for cp in w2[k]:
            cp.wait_recv()
    grad_in(0)
    own_z(0)
    near_far(1)
    far(2)
    near_own(2)
    grad_in(1)
    own_z(1)
    near_far(2)
    grad_in(2)
    far(3)
    near_own(3)
    own_z(2)
    near_far(3)
    grad_in(3)
    for off in range(3):
        rcopy(z_s.at[off], z_r.at[off], at(dz=1 + off), nst + 24 + off).wait_recv()
    own_part(3, (0, 1, 2))
    near_wait(3, 0)
    near_wait(3, 1)

    @pl.loop(0, FB // 128)
    def _(i):
        r = pl.ds(al(i * 128, 128), 128)
        tot = acc[r, :] + near_r[3, 0, r, :].astype(F32) + near_r[3, 1, r, :].astype(F32)
        fin[:, r] = tot.T.astype(BF)

    def drows(yy):
        return pl.ds(al((yy % 4) * rows_w, 16), rows_w)

    fcp = []
    for t, j in enumerate((2, 1, 3)):
        cp = rcopy(fin.at[drows(y + j), :], gd_out.at[:, fcols(y)], at(dy=j), nst + 33 + t)
        cp.start()
        fcp.append(cp)
    outs.append(lcopy(fin.at[drows(y), :], gd_out.at[:, fcols(y)]))

    for cp in sends:
        cp.wait_send()
    for cond, cp in zwhen:
        pl.when(cond)(cp.wait_send)
    for i in range(4):
        for cp in far_copies(i) + sum(near_copies(i), []):
            cp.wait_send()
    for i in range(3):
        z_copy(i).wait_send()
        for cp in out_copies(i):
            cp.wait()
        fcp[i].wait()
    for cp in outs:
        cp.wait()


def shards(go, gate, up, w):
    T, D = go.shape
    F = gate.shape[1]
    FB, DB = F // 4, w.shape[0] * 4
    vm = lambda *s: pltpu.VMEM(s, BF)
    return pl.pallas_call(
        functools.partial(kernel, T, D, FB, DB),
        out_shape=(
            jax.ShapeDtypeStruct((T, F), BF),
            jax.ShapeDtypeStruct((T, F), BF),
            jax.ShapeDtypeStruct(w.shape, BF),
        ),
        in_specs=[pl.BlockSpec(memory_space=pl.ANY)] * 4,
        out_specs=(pl.BlockSpec(memory_space=pl.ANY),) * 3,
        scratch_shapes=[
            vm(4 * T, 4 * D), vm(16 * DB, FB), vm(4 * T, FB), vm(4 * T, FB), vm(FB, 4 * T),
            pltpu.VMEM((T, FB), F32), vm(4, T, FB), vm(4, T, FB), pltpu.VMEM((FB, DB), F32),
            vm(4, 2, FB // 2, DB), vm(4, 2, FB // 2, DB), vm(4, 2, FB, DB), vm(4, 2, FB, DB),
            vm(3, FB, DB), vm(3, FB, DB), vm(DB, FB),
            pltpu.SemaphoreType.DMA((112,)), pltpu.SemaphoreType.DMA((112,)), pltpu.SemaphoreType.DMA((12,)),
        ],
        compiler_params=pltpu.CompilerParams(
            collective_id=0, has_side_effects=True, vmem_limit_bytes=58 << 20
        ),
        cost_estimate=pl.CostEstimate(
            flops=4 * 4 * T * 4 * D * FB, bytes_accessed=12 * T * F, transcendentals=2 * T * F
        ),
        name="regrouped_backward",
    )(go, gate, up, w)


def solution(mesh):
    fine = Mesh(mesh.devices.reshape(4, 4, 4, 2, 2), AXES)
    spec = P(("zl", "x", "y"), ("zh", "c"))
    return jax.shard_map(
        shards, mesh=fine, in_specs=(spec,) * 4, out_specs=(spec,) * 3, check_vma=False
    )
```

time: 180 us -> 165 us (0.917)
  Pallas kernels: 172 us -> 158 us
    pallas_call x1, Pallas kernels: 172 us -> 158 us  [shards(): pl.pallas_call(functools.partial(kernel, T, D, FB, DB), out_shape=(jax.Sh...]
where the time goes in v2:
time: 165 us; the launch traced here: 164 us
  Pallas kernels  158 us (96%)
  local copies, waits for them, and re-layouts  5.08 us (3%)
    pallas_call x1, Pallas kernels, shards(): pl.pallas_call(functools.partial(kernel, T, D, FB, DB), out_shape=(jax.Sh...  158 us
    unnamed x7, local copies, waits for them, and re-layouts  5.08 us

profile of v2, /device:TPU:96, one launch (start us, length us, event | category | flops | bytes accessed | tf_op | source)
XLA Modules:
  0.0 164.2 jit_solution(17788625822457516174)
XLA Ops:
  0.6 158.5 %regrouped_backward.1 = (bf16[256,3584]{1,0:T(8,128)(2,1)}, bf16[256,3584]{1,0:T(8,128)(2,1)}, bf16[64,3584]{1,0:T(8,128)(2,1)}) custom-call(bf16[256,1024]{1,0:T(8,128)(2,1)} %go_in.1, bf16[256,3584]{1,0:T(8,128)(2,1)} %gate_in.1, bf16[256,3584]{1,0:T(8,128)(2,1)} %up_in.1, bf16[64,3584]{1,0:T(8,128)(2,1)} %w_in.1), custom_call_target="tpu_custom_call" | custom-call | flops 15032385536 | bytes 11010048 | tf_op jit(solution)/shard_map/regrouped_backward/pallas_call | solution.py:395
  159.1 0.0 copy-start
  159.1 3.0 %copy.10 = bf16[256,3584]{1,0:T(8,128)(2,1)} copy(bf16[256,3584]{1,0:T(8,128)(2,1)} %get-tuple-element.6) | data formatting | bytes 3670016
  162.1 0.0 copy-done
  162.1 0.0 copy-start.1
  162.1 1.2 copy.11
  163.3 0.1 copy-done.1
  163.4 0.8 copy.12
Async XLA Ops:
  159.1 3.0 %copy-start = (bf16[256,3584]{1,0:T(8,128)(2,1)S(1)}, bf16[256,3584]{1,0:T(8,128)(2,1)}, u32[]{:S(2)}) copy-start(bf16[256,3584]{1,0:T(8,128)(2,1)} %get-tuple-element.7) | copy-start | bytes 5505028
  162.1 1.3 copy-start.1

commit v3 on v2

--- a/solution.py
+++ b/solution.py
@@ -20,7 +20,7 @@
     T, D, FB, DB,
     go_in, gate_in, up_in, w_in,
     gg_out, gu_out, gd_out,
-    go, w, gate, up, ht, gh, ggs, gus, acc,
+    go, w, gate, up, ht, hs, gh, ghs, ghr, acc,
     far_s, far_r, near_s, near_r, z_s, z_r, fin,
     ssem, rsem, lsem,
 ):
@@ -84,16 +84,10 @@
     my_w = pl.ds(al(((zl * 4 + x) * 4 + y) * rows_w, 16), rows_w)
     wy = [send(("wy", j), w_in.at[:, fcols(y + j)], w.at[my_w, :], at(dy=j)) for j in (1, 3, 2)]
     wl = lcopy(w_in.at[:, fcols(y)], w.at[my_w, :])
-    gul = (lcopy(gate_in.at[:, fcols(y)], gate.at[trows(y), :]),
-           lcopy(up_in.at[:, fcols(y)], up.at[trows(y), :]))
+    pieces = {j: (lcopy(gate_in.at[:, fcols(y + j)], gate.at[:, fcols(y + j)]),
+                  lcopy(up_in.at[:, fcols(y + j)], up.at[:, fcols(y + j)])) for j in (1, 3, 2, 0)}
     gl = lcopy(go_in, gblock(0, 0))
-    gu = {}
-    for j in (1, 3, 2):
-        gu[j] = (
-            send(("gate", j), gate_in.at[:, fcols(y + j)], gate.at[trows(y), :], at(dy=j)),
-            send(("up", j), up_in.at[:, fcols(y + j)], up.at[trows(y), :], at(dy=j)),
-        )
-    gcs = [send(("gc", 0, 0), go_in, gblock(0, 0), at(dc=1))]
+    gcs = {0: [send(("gc", 0, 0), go_in, gblock(0, 0), at(dc=1))], 1: []}
 
     def ring_sends(tag, ref, axis):
         out = {}
@@ -129,11 +123,22 @@
     def g_y_sends(s):
         g1[s] = ring_sends(("g", s), g_ref(s), "dy")
 
+    def g_y_half(s, k):
+        for i, sgn in enumerate("pm"):
+            g1.setdefault(s, {})[i, k] = send(("g", s, sgn, "h", k), gblock(s, 0, k), gblock(s, 0, k), at(dy=1 + 2 * i))
+
+    def g_y_forward1(s):
+        g1[s][0, 0].wait_recv()
+        a = send(("g", s, "fp"), gblock(s, -1, 0), gblock(s, -1, 0), at(dy=1))
+        g1[s][1, 1].wait_recv()
+        b = send(("g", s, "fm"), gblock(s, 1, 1), gblock(s, 1, 1), at(dy=3))
+        g2[s] = (g1[s][0, 1], g1[s][1, 0], a, b)
+
     def g_y_forward(s):
         g2[s] = ring_forward(("g", s), g_ref(s), "dy", g1[s])
 
     def g_core(s, tag, blk):
-        gcs.append(send(("gc", s, tag), blk, blk, at(dc=1)))
+        gcs[s].append(send(("gc", s, tag), blk, blk, at(dc=1)))
 
     def g_core_near(s):
         g2[s][0].wait_recv()
@@ -147,17 +152,21 @@
         g2[s][3].wait_recv()
         g_core(s, 5, gblock(s, 2, 1))
 
-    def hidden(yy):
-        r0 = trows(yy)
+    def hidden(j, ref):
+        for cp in pieces[j]:
+            cp.wait()
+        c0 = ((y + j) % 4) * FB
 
         @pl.loop(0, FB // 128)
         def _(i):
-            cs = pl.ds(al(i * 128, 128), 128)
-            g = gate[r0, cs].astype(F32)
-            u = up[r0, cs].astype(F32)
+            cs = pl.ds(al(c0 + i * 128, 128), 128)
+            g = gate[:, cs].astype(F32)
+            u = up[:, cs].astype(F32)
             h = g * jax.nn.sigmoid(g) * u
-            ht[cs, r0] = h.T.astype(BF)
-
+            ref[pl.ds(al(i * 128, 128), 128), :] = h.T.astype(BF)
+
+    hid = []
+    tcols = pl.ds(al(y * T, 128), T)
     wl.wait()
     for cp in wy:
         cp.wait_recv()
@@ -190,40 +199,35 @@
         dest = zl + 1 - 2 * r
         z_w_send(src, (dest + 4) % 4, 7 + k, j % 6, (dest >= 0) & (dest <= 3))
 
-    gz = [send(("gz", 0), go_in.at[pl.ds(0, half_t), :], gblock(0, 0, 0), at(dh=1))]
+    for t, j in enumerate((1, 3, 2)):
+        hidden(j, hs.at[t])
+        hid.append(send(("hid", j), hs.at[t], ht.at[:, tcols], at(dy=j)))
     gl.wait()
     g_y_sends(0)
-    for cp in gul:
-        cp.wait()
-    hidden(y)
+    hidden(0, ht.at[:, tcols])
     w_x_forward(0)
     z_w_slot(1)
     w_x_sends(1)
+    gz = [send(("gz", 0), go_in.at[pl.ds(0, half_t), :], gblock(0, 0, 0), at(dh=1))]
     z_w_slot(2)
     w_x_sends(2)
-    gz.append(send(("gz", 1), go_in.at[pl.ds(half_t, half_t), :], gblock(0, 0, 1), at(dh=1)))
     w_x_forward(1)
-    for cp in gu[1]:
-        cp.wait_recv()
-    hidden(y - 1)
-    for cp in gu[3]:
-        cp.wait_recv()
-    hidden(y - 3)
     z_w_slot(3)
     w_x_sends(3)
+    gz.append(send(("gz", 1), go_in.at[pl.ds(half_t, half_t), :], gblock(0, 0, 1), at(dh=1)))
+    g_y_forward(0)
     w_x_forward(2)
-    for cp in gu[2]:
+    g_core_near(0)
+    g_core_far(0)
+    gz[0].wait_recv()
+    g_y_half(1, 0)
+    gz[1].wait_recv()
+    g_y_half(1, 1)
+    g_core(1, 0, gblock(1, 0))
+    w_x_forward(3)
+    for cp in hid:
         cp.wait_recv()
-    hidden(y - 2)
-    g_y_forward(0)
-    w_x_forward(3)
-    for cp in gz:
-        cp.wait_recv()
-    g_y_sends(1)
-    g_core_near(0)
-    g_core(1, 0, gblock(1, 0))
-    g_core_far(0)
-    for cp in (gcs[i] for i in (0, 1, 2, 4, 5)):
+    for cp in gcs[0]:
         cp.wait_recv()
 
     nst = 72
@@ -292,43 +296,43 @@
 
     outs = []
 
-    def out_copies(t):
-        j = (2, 1, 3)[t]
-        return (
-            rcopy(ggs.at[t], gg_out.at[:, fcols(y)], at(dy=j), nst + 27 + t),
-            rcopy(gus.at[t], gu_out.at[:, fcols(y)], at(dy=j), nst + 30 + t),
-        )
-
-    def grad_in(t):
-        yy = y + (2, 1, 3, 0)[t]
-        r0 = al((yy % 4) * T, 16)
-        gh[...] = dot(go[pl.ds(r0, T), :], w[...])
+    def out_copy(t):
+        return rcopy(ghs.at[t], ghr.at[t], at(dy=(2, 1, 3)[t]), nst + 27 + t)
+
+    def grads(yy, ref):
+        cs = fcols(yy)
 
         @pl.loop(0, T // 32)
         def _(i):
             r = pl.ds(al(i * 32, 16), 32)
-            rr = pl.ds(al(r0 + i * 32, 16), 32)
-            g = gate[rr, :].astype(F32)
-            u = up[rr, :].astype(F32)
+            g = gate[r, cs].astype(F32)
+            u = up[r, cs].astype(F32)
             s = jax.nn.sigmoid(g)
-            d = gh[r, :]
-            ggs[t, r, :] = (d * u * s * (1.0 + g * (1.0 - s))).astype(BF)
-            gus[t, r, :] = (d * (g * s)).astype(BF)
-
+            d = ref[r, :].astype(F32)
+            gg_out[r, cs] = (d * u * s * (1.0 + g * (1.0 - s))).astype(BF)
+            gu_out[r, cs] = (d * (g * s)).astype(BF)
+
+    def grad_in(t):
+        yy = y + (2, 1, 3, 0)[t]
+        p = dot(go[pl.ds(al((yy % 4) * T, 16), T), :], w[...])
         if t < 3:
-            for cp in out_copies(t):
-                cp.start()
+            ghs[t] = p.astype(BF)
+            out_copy(t).start()
         else:
-            outs.append(lcopy(ggs.at[t], gg_out.at[:, fcols(y)]))
-            outs.append(lcopy(gus.at[t], gu_out.at[:, fcols(y)]))
+            gh[...] = p
+            grads(y, gh)
+
+    def grads_from(t):
+        out_copy(t).wait_recv()
+        grads(y - (2, 1, 3)[t], ghr.at[t])
 
     far(0)
     near_own(0)
-    g_y_forward(1)
+    g_y_forward1(1)
     near_far(0)
     g_core_near(1)
     g_core_far(1)
-    for cp in (gcs[i] for i in (3, 6, 7, 8, 9)):
+    for cp in gcs[1]:
         cp.wait_recv()
     far(1)
     near_own(1)
@@ -344,11 +348,14 @@
     own_z(1)
     near_far(2)
     grad_in(2)
+    grads_from(0)
     far(3)
     near_own(3)
     own_z(2)
     near_far(3)
     grad_in(3)
+    grads_from(1)
+    grads_from(2)
     for off in range(3):
         rcopy(z_s.at[off], z_r.at[off], at(dz=1 + off), nst + 24 + off).wait_recv()
     own_part(3, (0, 1, 2))
@@ -380,8 +387,7 @@
             cp.wait_send()
     for i in range(3):
         z_copy(i).wait_send()
-        for cp in out_copies(i):
-            cp.wait()
+        out_copy(i).wait_send()
         fcp[i].wait()
     for cp in outs:
         cp.wait()
@@ -395,21 +401,21 @@
     return pl.pallas_call(
         functools.partial(kernel, T, D, FB, DB),
         out_shape=(
-            jax.ShapeDtypeStruct((T, F), BF),
-            jax.ShapeDtypeStruct((T, F), BF),
-            jax.ShapeDtypeStruct(w.shape, BF),
+            pltpu.VMEM((T, F), BF),
+            pltpu.VMEM((T, F), BF),
+            pltpu.VMEM(w.shape, BF),
         ),
         in_specs=[pl.BlockSpec(memory_space=pl.ANY)] * 4,
-        out_specs=(pl.BlockSpec(memory_space=pl.ANY),) * 3,
+        out_specs=(pl.BlockSpec(memory_space=pltpu.VMEM),) * 3,
         scratch_shapes=[
-            vm(4 * T, 4 * D), vm(16 * DB, FB), vm(4 * T, FB), vm(4 * T, FB), vm(FB, 4 * T),
-            pltpu.VMEM((T, FB), F32), vm(4, T, FB), vm(4, T, FB), pltpu.VMEM((FB, DB), F32),
+            vm(4 * T, 4 * D), vm(16 * DB, FB), vm(T, F), vm(T, F), vm(FB, 4 * T), vm(3, FB, T),
+            pltpu.VMEM((T, FB), F32), vm(3, T, FB), vm(3, T, FB), pltpu.VMEM((FB, DB), F32),
             vm(4, 2, FB // 2, DB), vm(4, 2, FB // 2, DB), vm(4, 2, FB, DB), vm(4, 2, FB, DB),
             vm(3, FB, DB), vm(3, FB, DB), vm(DB, FB),
-            pltpu.SemaphoreType.DMA((112,)), pltpu.SemaphoreType.DMA((112,)), pltpu.SemaphoreType.DMA((12,)),
+            pltpu.SemaphoreType.DMA((112,)), pltpu.SemaphoreType.DMA((112,)), pltpu.SemaphoreType.DMA((16,)),
         ],
         compiler_params=pltpu.CompilerParams(
-            collective_id=0, has_side_effects=True, vmem_limit_bytes=58 << 20
+            collective_id=0, has_side_effects=True, vmem_limit_bytes=52 << 20
         ),
         cost_estimate=pl.CostEstimate(
             flops=4 * 4 * T * 4 * D * FB, bytes_accessed=12 * T * F, transcendentals=2 * T * F

time: 165 us -> 158 us (0.958)
  Pallas kernels: 158 us -> 154 us
  local copies, waits for them, and re-layouts: 5.08 us -> 3.23 us
    pallas_call x1, Pallas kernels: 158 us -> 154 us  [shards(): pl.pallas_call(functools.partial(kernel, T, D, FB, DB), out_shape=(pltpu....]
    unnamed x7 -> x3, local copies, waits for them, and re-layouts: 5.08 us -> 3.23 us
where the time goes in v3:
time: 158 us
  Pallas kernels  154 us (97%)
  local copies, waits for them, and re-layouts  3.23 us (2%)
    pallas_call x1, Pallas kernels, shards(): pl.pallas_call(functools.partial(kernel, T, D, FB, DB), out_shape=(pltpu....  154 us
    unnamed x3, local copies, waits for them, and re-layouts  3.23 us

profile of v3, /device:TPU:96, one launch (start us, length us, event | category | flops | bytes accessed | tf_op | source)
XLA Modules:
  0.0 158.0 jit_solution(15255589549205672381)
XLA Ops:
  0.6 154.1 %regrouped_backward.1 = (bf16[256,3584]{1,0:T(8,128)(2,1)S(1)}, bf16[256,3584]{1,0:T(8,128)(2,1)S(1)}, bf16[64,3584]{1,0:T(8,128)(2,1)S(1)}) custom-call(bf16[256,1024]{1,0:T(8,128)(2,1)} %go_in.1, bf16[256,3584]{1,0:T(8,128)(2,1)} %gate_in.1, bf16[256,3584]{1,0:T(8,128)(2,1)} %up_in.1, bf16[64,3584]{1,0:T(8,128)(2,1)} %w_in.1), custom_call_target="tpu_custom_call" | custom-call | flops 15032385536 | bytes 11010048 | tf_op jit(solution)/shard_map/regrouped_backward/pallas_call | solution.py:401
  154.8 1.2 copy.10
  156.0 0.8 copy.12
  156.8 1.2 copy.11

commit v4 on v3

--- a/solution.py
+++ b/solution.py
@@ -62,7 +62,6 @@
     bar = pltpu.get_barrier_semaphore()
     for p in partners:
         pl.semaphore_signal(bar, inc=1, device_id=p, device_id_type=pl.DeviceIdType.MESH)
-    pl.semaphore_wait(bar, len(partners))
 
     def fcols(yy):
         return pl.ds(al((yy % 4) * FB, 128), FB)
@@ -82,11 +81,12 @@
         return go.at[trows(y + dy, k), pl.ds(al(quarter(s) * D, 128), D)]
 
     my_w = pl.ds(al(((zl * 4 + x) * 4 + y) * rows_w, 16), rows_w)
-    wy = [send(("wy", j), w_in.at[:, fcols(y + j)], w.at[my_w, :], at(dy=j)) for j in (1, 3, 2)]
     wl = lcopy(w_in.at[:, fcols(y)], w.at[my_w, :])
     pieces = {j: (lcopy(gate_in.at[:, fcols(y + j)], gate.at[:, fcols(y + j)]),
                   lcopy(up_in.at[:, fcols(y + j)], up.at[:, fcols(y + j)])) for j in (1, 3, 2, 0)}
     gl = lcopy(go_in, gblock(0, 0))
+    pl.semaphore_wait(bar, len(partners))
+    wy = [send(("wy", j), w_in.at[:, fcols(y + j)], w.at[my_w, :], at(dy=j)) for j in (1, 3, 2)]
     gcs = {0: [send(("gc", 0, 0), go_in, gblock(0, 0), at(dc=1))], 1: []}
 
     def ring_sends(tag, ref, axis):
@@ -342,18 +342,18 @@
     grad_in(0)
     own_z(0)
     near_far(1)
+    grad_in(1)
     far(2)
     near_own(2)
-    grad_in(1)
+    grad_in(2)
     own_z(1)
     near_far(2)
-    grad_in(2)
-    grads_from(0)
+    grad_in(3)
     far(3)
     near_own(3)
     own_z(2)
     near_far(3)
-    grad_in(3)
+    grads_from(0)
     grads_from(1)
     grads_from(2)
     for off in range(3):

time: 158 us -> 158 us (level)
  no operation moved by 1% of the time
where the time goes in v4:
time: 158 us
  Pallas kernels  154 us (97%)
  local copies, waits for them, and re-layouts  3.23 us (2%)
    pallas_call x1, Pallas kernels, shards(): pl.pallas_call(functools.partial(kernel, T, D, FB, DB), out_shape=(pltpu....  154 us
    unnamed x3, local copies, waits for them, and re-layouts  3.23 us

profile of v4, /device:TPU:96, one launch (start us, length us, event | category | flops | bytes accessed | tf_op | source)
XLA Modules:
  0.0 158.0 jit_solution(12983557125628742029)
XLA Ops:
  0.6 154.1 %regrouped_backward.1 = (bf16[256,3584]{1,0:T(8,128)(2,1)S(1)}, bf16[256,3584]{1,0:T(8,128)(2,1)S(1)}, bf16[64,3584]{1,0:T(8,128)(2,1)S(1)}) custom-call(bf16[256,1024]{1,0:T(8,128)(2,1)} %go_in.1, bf16[256,3584]{1,0:T(8,128)(2,1)} %gate_in.1, bf16[256,3584]{1,0:T(8,128)(2,1)} %up_in.1, bf16[64,3584]{1,0:T(8,128)(2,1)} %w_in.1), custom_call_target="tpu_custom_call" | custom-call | flops 15032385536 | bytes 11010048 | tf_op jit(solution)/shard_map/regrouped_backward/pallas_call | solution.py:401
  154.7 1.2 copy.10
  156.0 0.8 copy.12
  156.7 1.2 copy.11
